TPU v7x, 32 devices: a whole 2x2x4 slice. The times are simulated.
32 devices in a mesh: gx: 4 (over y, core), gy: 4 (over z), gz: 2 (over x).
Axes of the slice: x: 2, y: 2, z: 4, core: 2. Of those that a mesh axis runs over, the one named last changes fastest.
Arguments:
- hidden_states: bfloat16 [2048, 8192], P(None, ('gx', 'gz')), may hold values from -9.5 to 9.5
- grad_out: bfloat16 [2048, 8192], P(None, ('gx', 'gz')), may hold values from -6 to 6
- query_weight: bfloat16 [8192, 8192], P(('gx', 'gz'), 'gy'), may hold values from -0.0625 to 0.0625
- key_weight: bfloat16 [8192, 1024], P(('gx', 'gz'), 'gy'), may hold values from -0.0625 to 0.0625
- value_weight: bfloat16 [8192, 1024], P(('gx', 'gz'), 'gy'), may hold values from -0.0625 to 0.0625
- output_weight: bfloat16 [8192, 8192], P('gy', ('gx', 'gz')), may hold values from -0.0625 to 0.0625
- segment_ids: int32 [2048], P('gz'), may hold values from 0 to 3, as said below
- positions: int32 [2048], P('gz'), may hold values from 0 to 767, as said below
Outputs:
- input_grad: bfloat16 [2048, 8192], P('gy', ('gx', 'gz'))
- query_weight_grad: bfloat16 [8192, 8192], P(('gx', 'gz'), 'gy')
- key_weight_grad: bfloat16 [8192, 1024], P(('gx', 'gz'), 'gy')
- value_weight_grad: bfloat16 [8192, 1024], P(('gx', 'gz'), 'gy')
- output_weight_grad: bfloat16 [8192, 8192], P('gy', ('gx', 'gz'))
Inputs may be any that keep to these rules, and one draw needn't show every extreme that they name: `segment_ids`: tokens come in aligned blocks of 1024; block b holds a chosen sequence with id 2 b followed by its rejected sequence with id 2 b + 1, each of 256 tokens or more. Within each sequence the positions run 0, 1, 2, ... in token order.
All inputs are finite; a program needn't handle non-finite values.
Results may differ from a plain program's by a relative error of at most 0.03.
Values may be sent and summed in bfloat16 or wider, within the bound.
A program may use at most 192 MiB of HBM per device.

v0:
```python
import math

import jax
import jax.numpy as jnp
from jax import lax
from jax.sharding import PartitionSpec as P

HD = 128


rope_base = 10000.0
masked_score = -1e30


def rope_tables(positions, head_size):
    halves = jnp.arange(head_size // 2, dtype=jnp.float32)
    inverse = rope_base ** (-2.0 * halves / head_size)
    angles = positions.astype(jnp.float32)[:, None] * inverse[None, :]
    return (jnp.cos(angles), jnp.sin(angles))


def rotate(values, cosine, sine, direction):
    middle = values.shape[-1] // 2
    leading = values[..., :middle]
    trailing = values[..., middle:]
    cosine_b = cosine[:, None, :]
    sine_b = sine[:, None, :] * direction
    return jnp.concatenate(
        [leading * cosine_b - trailing * sine_b, trailing * cosine_b + leading * sine_b], axis=-1
    )


def rounded_term(term):
    return lax.optimization_barrier(term.astype(jnp.bfloat16)).astype(jnp.float32)


def per_device(
    hidden_states,
    grad_out,
    query_weight,
    key_weight,
    value_weight,
    output_weight,
    segment_ids,
    positions,
):
    across = lax.axis_size("gx")
    depth_count = lax.axis_size("gz")
    token_count, breadth = hidden_states.shape
    block_rows = token_count // depth_count
    head_size = HD
    columns = query_weight.shape[1] // across
    heads_here = columns // head_size
    kv_groups = key_weight.shape[1] // head_size
    scale = 1.0 / math.sqrt(head_size)
    hidden_blocks = hidden_states.reshape(depth_count, block_rows, breadth)
    grad_blocks = grad_out.reshape(depth_count, block_rows, breadth)
    query_groups = query_weight.reshape(breadth, across, columns)
    output_groups = output_weight.reshape(across, columns, breadth)
    number = lax.axis_size(("gx", "gz")) * block_rows // block_rows
    chosen = jnp.arange(number, dtype=jnp.int32)
    source_rows = jnp.take(hidden_blocks, chosen % depth_count, axis=0)
    weight_cols = jnp.take(query_groups, chosen // depth_count, axis=1)
    product = jnp.einsum(
        "bta,abc->btc", source_rows, weight_cols, preferred_element_type=jnp.float32
    )
    query = lax.psum_scatter(
        rounded_term(product.reshape(lax.axis_size(("gx", "gz")) * block_rows, columns)),
        ("gx", "gz"),
        scatter_dimension=0,
        tiled=True,
    )
    number = lax.axis_size(("gx", "gz")) * block_rows // block_rows
    chosen = jnp.arange(number, dtype=jnp.int32)
    source_rows = jnp.take(grad_blocks, chosen % depth_count, axis=0)
    weight_rows = jnp.take(output_groups, chosen // depth_count, axis=0)
    product = jnp.einsum(
        "bta,bca->btc", source_rows, weight_rows, preferred_element_type=jnp.float32
    )
    grad_heads = lax.psum_scatter(
        rounded_term(product.reshape(lax.axis_size(("gx", "gz")) * block_rows, columns)),
        ("gx", "gz"),
        scatter_dimension=0,
        tiled=True,
    )
    key_partial = rounded_term(
        jnp.dot(hidden_states, key_weight, preferred_element_type=jnp.float32)
    )
    value_partial = rounded_term(
        jnp.dot(hidden_states, value_weight, preferred_element_type=jnp.float32)
    )
    key_all, value_all = lax.psum((key_partial, value_partial), ("gx", "gz"))
    block_index = lax.axis_index("gz")
    key_block = lax.dynamic_slice_in_dim(key_all, block_index * block_rows, block_rows, 0)
    value_block = lax.dynamic_slice_in_dim(value_all, block_index * block_rows, block_rows, 0)
    member = lax.axis_index("gx")
    shared_index = member // (across // kv_groups)
    cosine, sine = rope_tables(positions, head_size)
    query_rot = rotate(query.reshape(block_rows, heads_here, head_size), cosine, sine, 1.0).astype(
        jnp.bfloat16
    )
    key_one = lax.dynamic_slice_in_dim(key_block, shared_index * head_size, head_size, 1)
    key_rot = (
        rotate(key_one.reshape(block_rows, 1, head_size), cosine, sine, 1.0)
        .reshape(block_rows, head_size)
        .astype(jnp.bfloat16)
    )
    value_low = lax.dynamic_slice_in_dim(
        value_block, shared_index * head_size, head_size, 1
    ).astype(jnp.bfloat16)
    grad_low = grad_heads.reshape(block_rows, heads_here, head_size).astype(jnp.bfloat16)
    allowed = (segment_ids[:, None] == segment_ids[None, :]) & (
        positions[None, :] <= positions[:, None]
    )
    scores = (
        jnp.einsum("qhd,kd->hqk", query_rot, key_rot, preferred_element_type=jnp.float32) * scale
    )
    scores = jnp.where(allowed[None], scores, masked_score)
    largest = jnp.max(scores, axis=-1, keepdims=True)
    weights = jnp.exp(scores - largest)
    probs = weights / jnp.sum(weights, axis=-1, keepdims=True)
    probs_low = probs.astype(jnp.bfloat16)
    outputs = jnp.einsum(
        "hqk,kd->qhd", probs_low, value_low, preferred_element_type=jnp.float32
    ).astype(jnp.bfloat16)
    delta = jnp.sum(grad_low.astype(jnp.float32) * outputs.astype(jnp.float32), axis=-1)
    dprob = jnp.einsum("qhd,kd->hqk", grad_low, value_low, preferred_element_type=jnp.float32)
    dscore = (probs * (dprob - delta.T[:, :, None])).astype(jnp.bfloat16)
    dquery = jnp.einsum("hqk,kd->qhd", dscore, key_rot, preferred_element_type=jnp.float32) * scale
    dkey = jnp.einsum("hqk,qhd->khd", dscore, query_rot, preferred_element_type=jnp.float32) * scale
    dvalue = jnp.einsum("hqk,qhd->khd", probs_low, grad_low, preferred_element_type=jnp.float32)
    dquery_low = (
        rotate(dquery, cosine, sine, -1.0).astype(jnp.bfloat16).reshape(block_rows, columns)
    )
    dkey_low = rotate(dkey, cosine, sine, -1.0).astype(jnp.bfloat16).reshape(block_rows, columns)
    dvalue_low = dvalue.astype(jnp.bfloat16).reshape(block_rows, columns)
    output_flat = outputs.reshape(block_rows, columns)
    outputs_all = lax.all_gather(output_flat, ("gx", "gz"), axis=0, tiled=True)
    outputs_groups = outputs_all.reshape(across, token_count, columns)
    dquery_all, key_each, value_each = (
        lax.all_gather(dquery_low, ("gx", "gz"), axis=0, tiled=True),
        lax.all_gather(dkey_low, ("gx", "gz"), axis=0, tiled=True),
        lax.all_gather(dvalue_low, ("gx", "gz"), axis=0, tiled=True),
    )
    sharers = across // kv_groups
    key_grads = (
        key_each.reshape(kv_groups, sharers, token_count, heads_here, head_size)
        .astype(jnp.float32)
        .sum(axis=(1, 3))
        .astype(jnp.bfloat16)
        .transpose(1, 0, 2)
    )
    value_grads = (
        value_each.reshape(kv_groups, sharers, token_count, heads_here, head_size)
        .astype(jnp.float32)
        .sum(axis=(1, 3))
        .astype(jnp.bfloat16)
        .transpose(1, 0, 2)
    )
    dquery_groups = dquery_all.reshape(across, token_count, columns)
    key_heads = key_weight.reshape(breadth, kv_groups, head_size)
    value_heads = value_weight.reshape(breadth, kv_groups, head_size)
    summed = jnp.einsum(
        "gtc,agc->ta", dquery_groups, query_groups, preferred_element_type=jnp.float32
    )
    summed = summed + jnp.einsum(
        "tkd,akd->ta", key_grads, key_heads, preferred_element_type=jnp.float32
    )
    summed = summed + jnp.einsum(
        "tkd,akd->ta", value_grads, value_heads, preferred_element_type=jnp.float32
    )
    input_grad = lax.psum_scatter(
        rounded_term(summed), "gy", scatter_dimension=0, tiled=True
    ).astype(jnp.bfloat16)
    query_weight_grad = (
        jnp.einsum("ta,gtc->agc", hidden_states, dquery_groups, preferred_element_type=jnp.float32)
        .reshape(breadth, across * columns)
        .astype(jnp.bfloat16)
    )
    key_weight_grad = (
        jnp.einsum("ta,tkd->akd", hidden_states, key_grads, preferred_element_type=jnp.float32)
        .reshape(breadth, kv_groups * head_size)
        .astype(jnp.bfloat16)
    )
    value_weight_grad = (
        jnp.einsum("ta,tkd->akd", hidden_states, value_grads, preferred_element_type=jnp.float32)
        .reshape(breadth, kv_groups * head_size)
        .astype(jnp.bfloat16)
    )
    output_weight_grad = (
        jnp.einsum("gtc,ta->gca", outputs_groups, grad_out, preferred_element_type=jnp.float32)
        .reshape(across * columns, breadth)
        .astype(jnp.bfloat16)
    )
    return (input_grad, query_weight_grad, key_weight_grad, value_weight_grad, output_weight_grad)


def solution(mesh):
    placed = (
        P(None, ("gx", "gz")),
        P(None, ("gx", "gz")),
        P(("gx", "gz"), "gy"),
        P(("gx", "gz"), "gy"),
        P(("gx", "gz"), "gy"),
        P("gy", ("gx", "gz")),
        P("gz"),
        P("gz"),
    )
    return jax.shard_map(
        per_device,
        mesh=mesh,
        in_specs=placed,
        out_specs=(
            P("gy", ("gx", "gz")),
            P(("gx", "gz"), "gy"),
            P(("gx", "gz"), "gy"),
            P(("gx", "gz"), "gy"),
            P("gy", ("gx", "gz")),
        ),
        check_vma=False,
    )
```

profile of v0, /device:TPU:0, one launch (start us, length us, event | category | flops | bytes accessed | tf_op | source)
XLA Modules:
  0.0 655.6 jit_solution(9989080963153840186)
XLA Ops:
  11.5 6.0 gather_fusion.5
  21.9 6.9 %gather_fusion.1 = bf16[8,512,1024]{2,1,0:T(8,128)(2,1)} fusion(bf16[4,512,1024]{2,1,0:T(8,128)(2,1)} %bitcast.145, s32[1024]{0:T(1024)S(1)} %pad_clamp_fusion), kind=kCustom, calls=%fused_computation.5 | custom fusion | bytes 16777248 | tf_op jit(solution)/shard_map/jit(_take)/gather | solution.py:76
  28.8 16.2 %fusion.23 = bf16[8,1024,512]{2,1,0:T(8,128)(2,1)} fusion(bf16[8,512,1024]{2,1,0:T(8,128)(2,1)} %gather_fusion.1, pred[8]{0:T(512)(128)(4,1)S(1)} %get-tuple-element.55, bf16[8,512,1024]{2,1,0:T(8,128)(2,1)} %gather_fusion.5, bf16[8,512,1024]{2,1,0:T(8,128)(2,1)} %gather_fusion.4, pred[8]{0:T(512)(128)(4,1)S(1)} %get-tuple-element.54), kind=kOutput, calls=%fused_computation.37 | convolution fusion | flops 8640266240 | bytes 33554448 | tf_op jit(solution)/shard_map/bta,bca->btc/dot_general | solution.py:77
  45.3 6.4 copy.124
  51.7 8.6 %gather_fusion = bf16[8,1024,512]{1,2,0:T(8,128)(2,1)} fusion(bf16[1024,4,512]{0,2,1:T(8,128)(2,1)} %bitcast.143, s32[1024]{0:T(1024)S(1)} %pad_clamp_fusion), kind=kCustom, calls=%fused_computation.4 | custom fusion | bytes 16777248 | tf_op jit(solution)/shard_map/jit(_take)/gather | solution.py:63
  60.3 5.0 fusion.83
  65.3 6.0 gather_fusion.3
  75.8 16.4 %fusion.26 = bf16[8,1024,512]{2,1,0:T(8,128)(2,1)} fusion(bf16[8,1024,512]{1,2,0:T(8,128)(2,1)} %gather_fusion, pred[8]{0:T(512)(128)(4,1)S(1)} %get-tuple-element.55, bf16[8,512,1024]{2,1,0:T(8,128)(2,1)} %gather_fusion.3, bf16[8,512,1024]{2,1,0:T(8,128)(2,1)} %gather_fusion.2, pred[8]{0:T(512)(128)(4,1)S(1)} %get-tuple-element.54), kind=kOutput, calls=%fused_computation.38 | convolution fusion | flops 8640266240 | bytes 33554448 | tf_op jit(solution)/shard_map/bta,abc->btc/dot_general | solution.py:64
  92.2 11.8 %copy.126 = bf16[8192,512]{0,1:T(8,128)(2,1)} copy(bf16[8192,512]{1,0:T(8,128)(2,1)} %bitcast.152) | data formatting | bytes 16777216 | tf_op jit(solution)/shard_map/optimization_barrier | solution.py:34
  104.0 11.6 %convert_element_type.130 = f32[8192,512]{0,1:T(8,128)} convert(bf16[8192,512]{0,1:T(8,128)(2,1)} %copy.126) | non-fusion elementwise | flops 4194304 | bytes 25165824 | tf_op jit(solution)/shard_map/convert_element_type | solution.py:34
  126.8 130.6 %all-reduce.4 = f32[2048,256]{1,0:T(8,128)S(1)} all-reduce(bf16[2048,256]{1,0:T(8,128)(2,1)} %convolution_convert_fusion.2), channel_id=1, replica_groups=mesh['gx'=4,'gy'=4,'gz'=2] {'gx','gz'}, use_global_device_ids=true, to_apply=%region_0.1 | all-reduce | flops 524288 | bytes 3145728 | tf_op jit(solution)/shard_map/psum | solution.py:92
  263.6 19.8 %reduce-scatter.4.cloned.1.call-done = f32[1024,512]{0,1:T(8,128)} async-done(((f32[8192,512]{0,1:T(8,128)}), f32[1024,512]{0,1:T(8,128)}) %reduce-scatter.4.cloned.1.call-update) | async-done | bytes 2097168 | tf_op jit(solution)/shard_map/reduce_scatter | solution.py:67
  295.2 11.4 %fusion.86 = (f32[4,1024]{1,0:T(4,128)S(1)}, f32[4,1024,1024]{1,2,0:T(8,128)}) fusion(pred[1024,1024]{0,1:T(8,128)(4,1)} %compare_and_fusion, bf16[1024,1,64]{0,2,1:T(8,128)(2,1)S(1)} %get-tuple-element.46, bf16[1024,1,64]{0,2,1:T(8,128)(2,1)S(1)} %get-tuple-element.45, bf16[1024,4,64]{2,0,1:T(8,128)(2,1)} %get-tuple-element.32, ...), kind=kOutput, calls=%fused_computation.127 | convolution fusion | flops 1093141504 | bytes 19152896 | tf_op jit(solution)/shard_map/sub | solution.py:120
  306.5 7.0 %fusion.29 = bf16[4,1024,1024]{1,2,0:T(8,128)(2,1)S(1)} fusion(f32[4,1024,1024]{1,2,0:T(8,128)} %get-tuple-element.51, f32[4,1024]{1,0:T(4,128)S(1)} %get-tuple-element.50), kind=kLoop, calls=%fused_computation.39 | loop fusion | flops 8388608 | bytes 25182208 | tf_op jit(solution)/shard_map/convert_element_type | solution.py:122
  321.0 22.5 %all-reduce.3.cloned.1.call-done = bf16[2048,256]{1,0:T(8,128)(2,1)} async-done(((bf16[2048,256]{1,0:T(8,128)(2,1)}), bf16[2048,256]{1,0:T(8,128)(2,1)}) %all-reduce.3.cloned.1.call-update) | async-done | bytes 1048592 | tf_op jit(solution)/shard_map/psum | solution.py:92
  343.5 6.1 multiply_reduce_fusion
  349.6 8.3 %fusion.8 = bf16[4,1024,1024]{1,2,0:T(8,128)(2,1)S(1)} fusion(bf16[1024,4,128]{0,2,1:T(8,128)(2,1)S(1)} %bitcast.147, f32[4,1024]{1,0:T(4,128)S(1)} %bitcast.169, f32[4,1024,1024]{1,2,0:T(8,128)} %get-tuple-element.51, f32[4,1024]{1,0:T(4,128)S(1)} %get-tuple-element.50, bf16[2048,256]{1,0:T(8,128)(2,1)} %all-reduce.3.cloned.1.call-done, s32[]{:T(128)S(6)} %select_n.88, ...), kind=kOutput, calls=%fused_computation.17 | convolution fusion | flops 1090519040 | bytes 26509320 | tf_op jit(solution)/shard_map/qhd,kd->hqk/dot_general | solution.py:127
  374.0 25.4 %all-gather.9.cloned.1.call-done = bf16[8192,512]{0,1:T(8,128)(2,1)} async-done(((bf16[1024,512]{0,1:T(8,128)(2,1)}), bf16[8192,512]{0,1:T(8,128)(2,1)}) %all-gather.9.cloned.1.call-update) | async-done | bytes 8388624 | tf_op jit(solution)/shard_map/all_gather | solution.py:143
  399.5 14.7 %reshape.313 = bf16[2,2,2048,4,128]{2,1,0,4,3:T(2,128)(2,1)} reshape(bf16[8192,512]{0,1:T(8,128)(2,1)} %all-gather.9.cloned.1.call-done) | data formatting | bytes 16777216 | tf_op jit(solution)/shard_map/reshape | solution.py:154
  414.1 13.4 %reduce_sum.45 = bf16[2,2048,128]{1,0,2:T(2,128)(2,1)S(1)} reduce(bf16[2,2,2048,4,128]{2,1,0,4,3:T(2,128)(2,1)} %reshape.313, bf16[]{:T(256)} %constant.140.clone.1), dimensions={1,3}, to_apply=%region_8.10 | reduce | flops 3670016 | bytes 9437186 | tf_op jit(solution)/shard_map/reduce_sum | solution.py:156
  427.5 28.3 %all-gather.7.cloned.1.call-done = bf16[8192,512]{0,1:T(8,128)(2,1)} async-done(((bf16[1024,512]{0,1:T(8,128)(2,1)}), bf16[8192,512]{0,1:T(8,128)(2,1)}) %all-gather.7.cloned.1.call-update) | async-done | bytes 8388624 | tf_op jit(solution)/shard_map/all_gather | solution.py:142
  455.8 14.7 %reshape.310 = bf16[2,2,2048,4,128]{2,1,0,4,3:T(2,128)(2,1)} reshape(bf16[8192,512]{0,1:T(8,128)(2,1)} %all-gather.7.cloned.1.call-done) | data formatting | bytes 16777216 | tf_op jit(solution)/shard_map/reshape | solution.py:147
  470.5 13.4 %reduce_sum.44 = bf16[2,2048,128]{1,0,2:T(2,128)(2,1)S(1)} reduce(bf16[2,2,2048,4,128]{2,1,0,4,3:T(2,128)(2,1)} %reshape.310, bf16[]{:T(256)} %constant.140.clone.1), dimensions={1,3}, to_apply=%region_7.9 | reduce | flops 3670016 | bytes 9437186 | tf_op jit(solution)/shard_map/reduce_sum | solution.py:149
  483.9 28.2 %all-gather.5.cloned.1.call-done = bf16[8192,512]{0,1:T(8,128)(2,1)} async-done(((bf16[1024,512]{0,1:T(8,128)(2,1)}), bf16[8192,512]{0,1:T(8,128)(2,1)}) %all-gather.5.cloned.1.call-update) | async-done | bytes 8388624 | tf_op jit(solution)/shard_map/all_gather | solution.py:141
  512.1 12.0 %copy.137 = bf16[8192,512]{1,0:T(8,128)(2,1)} copy(bf16[8192,512]{0,1:T(8,128)(2,1)} %all-gather.5.cloned.1.call-done) | data formatting | bytes 16777216 | tf_op jit(solution)/shard_map/all_gather | solution.py:141
  525.6 4.6 fusion.52
  530.2 15.2 %fusion.12 = bf16[2048,1024]{1,0:T(8,128)(2,1)} fusion(f32[2048,1024,1]{1,0,2:T(8,128)S(1)} %fusion.49, f32[2048,1024,1]{1,0,2:T(8,128)} %fusion.52, bf16[4,2048,512]{2,1,0:T(8,128)(2,1)} %bitcast.150, bf16[1024,4,512]{0,2,1:T(8,128)(2,1)S(1)} %bitcast.144), kind=kOutput, calls=%fused_computation.24 | convolution fusion | flops 8596226048 | bytes 33554432 | tf_op jit(solution)/shard_map/gtc,agc->ta/dot_general | solution.py:163
  545.4 14.2 %fusion.38 = bf16[4,512,1024]{2,1,0:T(8,128)(2,1)} fusion(bf16[4,2048,512]{2,1,0:T(8,128)(2,1)} %bitcast.151, bf16[2048,1024]{1,0:T(8,128)(2,1)} %param.10), kind=kOutput, calls=%fused_computation.50 | convolution fusion | flops 8592031744 | bytes 16777216 | tf_op jit(solution)/shard_map/ta,gtc->agc/dot_general | solution.py:176
  559.6 6.5 copy.153
  575.1 11.5 %copy.152 = bf16[4,512,2048]{2,1,0:T(8,128)(2,1)} copy(bf16[4,512,2048]{1,2,0:T(8,128)(2,1)} %bitcast.149) | data formatting | bytes 16777216 | tf_op jit(solution)/shard_map/gtc,ta->gca/dot_general | solution.py:191
  586.7 13.8 %convolution_convert_fusion = bf16[2048,1024]{1,0:T(8,128)(2,1)} fusion(bf16[2048,2048]{1,0:T(8,128)(2,1)} %bitcast.153, bf16[2048,1024]{1,0:T(8,128)(2,1)} %param.11), kind=kOutput, calls=%fused_computation.49 | convolution fusion | flops 8592031744 | bytes 16777216 | tf_op jit(solution)/shard_map/gtc,ta->gca/dot_general | solution.py:191
  600.5 47.9 %reduce-scatter.8.cloned.1.call-done = bf16[512,1024]{1,0:T(8,128)(2,1)} async-done(((bf16[2048,1024]{1,0:T(8,128)(2,1)}), bf16[512,1024]{1,0:T(8,128)(2,1)}) %reduce-scatter.8.cloned.1.call-update) | async-done | bytes 1048592 | tf_op jit(solution)/shard_map/reduce_scatter | solution.py:172
  (72 shorter events, 76.4 us)
Async XLA Ops:
  7.2 108.5 %copy-start = (bf16[1024,256]{1,0:T(8,128)(2,1)S(1)}, bf16[1024,256]{1,0:T(8,128)(2,1)}, u32[]{:S(2)}) copy-start(bf16[1024,256]{1,0:T(8,128)(2,1)} %param.14) | copy-start | bytes 1572868
  7.2 254.9 %reduce-scatter.6.cloned.1.call-start = ((), (), s32[]{:S(2)}) async-start(), calls=%async_computation.5 | async-start | bytes 9437184 | tf_op jit(solution)/shard_map/reduce_scatter | solution.py:80
  45.0 238.3 %reduce-scatter.4.cloned.1.call-start = ((), (), s32[]{:S(2)}) async-start(), calls=%async_computation.3 | async-start | bytes 18874368 | tf_op jit(solution)/shard_map/reduce_scatter | solution.py:67
  115.6 4.8 copy-start.7
  115.6 4.8 copy-start.8
  115.6 6.7 %copy-start.5 = (bf16[1024,256]{1,0:T(8,128)(2,1)S(1)}, bf16[1024,256]{1,0:T(8,128)(2,1)}, u32[]{:S(2)}) copy-start(bf16[1024,256]{1,0:T(8,128)(2,1)} %param.13) | copy-start | bytes 1572868
  115.7 227.8 %all-reduce.3.cloned.1.call-start = ((), (), s32[]{:S(2)}) async-start(), calls=%async_computation.4 | async-start | bytes 2097152 | tf_op jit(solution)/shard_map/psum | solution.py:92
  120.3 279.1 %all-gather.9.cloned.1.call-start = ((), (), s32[]{:S(2)}) async-start(), calls=%async_computation.8 | async-start | bytes 9437184 | tf_op jit(solution)/shard_map/all_gather | solution.py:143
  313.6 3.2 copy-start.1
  320.7 135.1 %all-gather.7.cloned.1.call-start = ((), (), s32[]{:S(2)}) async-start(), calls=%async_computation.7 | async-start | bytes 9437184 | tf_op jit(solution)/shard_map/all_gather | solution.py:142
  357.9 3.4 copy-start.4
  361.4 2.4 copy-start.3
  368.2 144.0 %all-gather.5.cloned.1.call-start = ((), (), s32[]{:S(2)}) async-start(), calls=%async_computation.6 | async-start | bytes 9437184 | tf_op jit(solution)/shard_map/all_gather | solution.py:141
  371.4 203.8 %all-gather.11.cloned.1.call-start = ((), (), s32[]{:S(2)}) async-start(), calls=%async_computation.10 | async-start | bytes 9437184 | tf_op jit(solution)/shard_map/all_gather | solution.py:138
  374.0 274.4 %reduce-scatter.8.cloned.1.call-start = ((), (), s32[]{:S(2)}) async-start(), calls=%async_computation.9 | async-start | bytes 5242880 | tf_op jit(solution)/shard_map/reduce_scatter | solution.py:172
  524.2 1.4 copy-start.6
  525.5 4.6 copy-start.2
Sparse Core Ops, SparseCore 0:
  45.1 73.9 reduce-scatter.5
  123.1 160.1 reduce-scatter.3
  286.8 56.6 all-reduce.2
  346.0 53.4 all-gather.8
  401.4 54.3 all-gather.6
  457.7 54.3 all-gather.4
  514.2 54.3 all-gather.10
  571.6 76.7 reduce-scatter.7
where the time goes:
time: 663 us; the launch traced here: 656 us
  waiting for transfers between devices  172 us (26%)
  local copies, waits for them, and re-layouts  143 us (22%)
  matrix products  133 us (20%)
  blocking collectives  131 us (20%)
  other arithmetic  60.5 us (9%)
  between operations  14.9 us (2%)
    psum x1, blocking collectives, per_device(): key_all, value_all = lax.psum((key_partial, value_partial), ('gx', 'gz'))  131 us
    reduce_scatter x1, waiting for transfers between devices, per_device(): lax.psum_scatter(rounded_term(summed), 'gy', scatter_dimension=0, tiled=T...  47.9 us
    all_gather x1, waiting for transfers between devices, per_device(): lax.all_gather(dkey_low, ('gx', 'gz'), axis=0, tiled=True)  28.3 us
    all_gather x1, waiting for transfers between devices, per_device(): lax.all_gather(dquery_low, ('gx', 'gz'), axis=0, tiled=True)  28.2 us
    all_gather x1, waiting for transfers between devices, per_device(): lax.all_gather(dvalue_low, ('gx', 'gz'), axis=0, tiled=True)  25.4 us
    unnamed x24, local copies, waits for them, and re-layouts  23.2 us
    psum x1, waiting for transfers between devices, per_device(): key_all, value_all = lax.psum((key_partial, value_partial), ('gx', 'gz'))  22.5 us
    reduce_scatter x2, waiting for transfers between devices, per_device(): lax.psum_scatter(rounded_term(product.reshape(lax.axis_size(('gx', 'gz'))...  19.8 us
  transfers between devices with their start and end apart: 8, of which 6 were waited for; matrix products, arithmetic and copies ran while one was open for 45% of the time, Pallas kernels for 0%

commit v1 on v0

v1 whole, which is shorter than its diff:
```python
import functools
import math

import jax
import jax.numpy as jnp
from jax import lax
from jax.experimental import pallas as pl
from jax.experimental.pallas import tpu as pltpu
from jax.sharding import PartitionSpec as P

HD = 128
GROUP = ("gx", "gz")

rope_base = 10000.0
masked_score = -1e30
VMEM_LIMIT = 56 * 1024 * 1024


def params():
    return pltpu.CompilerParams(vmem_limit_bytes=VMEM_LIMIT)


def cost(flops, moved):
    return pl.CostEstimate(flops=flops, bytes_accessed=moved, transcendentals=0)


def dot(a, b, ca, cb):
    return lax.dot_general(a, b, (((ca,), (cb,)), ((), ())), preferred_element_type=jnp.float32)


def rope_tables(positions, head_size):
    halves = jnp.arange(head_size // 2, dtype=jnp.float32)
    inverse = rope_base ** (-2.0 * halves / head_size)
    angles = positions.astype(jnp.float32)[:, None] * inverse[None, :]
    cosine, sine = jnp.cos(angles), jnp.sin(angles)
    return jnp.concatenate([cosine, cosine], axis=1), jnp.concatenate([-sine, sine], axis=1)


def rotate(values, cosine, sine):
    return values * cosine + pltpu.roll(values, values.shape[-1] // 2, 1) * sine


def project_kernel(x_ref, w_ref, o_ref, *, contract):
    o_ref[...] = dot(x_ref[...], w_ref[...], 1, contract).astype(o_ref.dtype)


def project(x, weight, across, transposed):
    tokens, depth = x.shape
    columns = weight.shape[0 if transposed else 1] // across
    tile = min(512, tokens)
    steps = tokens // tile
    if transposed:
        w_spec = pl.BlockSpec((columns, depth), lambda m, t: (m, 0))
    else:
        w_spec = pl.BlockSpec((depth, columns), lambda m, t: (0, m))
    return pl.pallas_call(
        functools.partial(project_kernel, contract=1 if transposed else 0),
        grid=(across, steps),
        out_shape=jax.ShapeDtypeStruct((across * tokens, columns), jnp.bfloat16),
        in_specs=[pl.BlockSpec((tile, depth), lambda m, t: (t, 0)), w_spec],
        out_specs=pl.BlockSpec((tile, columns), lambda m, t: (m * steps + t, 0)),
        compiler_params=params(),
        cost_estimate=cost(2 * tokens * depth * columns * across, 16 * 2**20),
    )(x, weight)


def project_kv_kernel(x_ref, k_ref, v_ref, o_ref):
    x = x_ref[...]
    o_ref[:, :HD] = dot(x, k_ref[...], 1, 0).astype(o_ref.dtype)
    o_ref[:, HD:] = dot(x, v_ref[...], 1, 0).astype(o_ref.dtype)


def project_kv(x, key_weight, value_weight, sharers, depth_count):
    tokens, depth = x.shape
    kv_groups = key_weight.shape[1] // HD
    rows = tokens // depth_count // sharers
    w_spec = pl.BlockSpec((depth, HD), lambda g, s, z: (0, g))
    return pl.pallas_call(
        project_kv_kernel,
        grid=(kv_groups, sharers, depth_count),
        out_shape=jax.ShapeDtypeStruct((kv_groups * tokens, 2 * HD), jnp.bfloat16),
        in_specs=[
            pl.BlockSpec((rows, depth), lambda g, s, z: (z * sharers + s, 0)),
            w_spec,
            w_spec,
        ],
        out_specs=pl.BlockSpec(
            (rows, 2 * HD), lambda g, s, z: ((g * sharers + s) * depth_count + z, 0)
        ),
        compiler_params=params(),
        cost_estimate=cost(4 * tokens * depth * HD * kv_groups, 8 * 2**20),
    )(x, key_weight, value_weight)


def attend_kernel(
    q_ref, g_ref, kv_ref, cos_ref, sin_ref, seg_col, seg_row, o_ref, dq_ref, dkv_ref, dk_acc, dv_acc, kr_ref, *, tile
):
    head = pl.program_id(0)
    rows = q_ref.shape[0]
    scale = 1.0 / math.sqrt(HD)

    @pl.when(head == 0)
    def _():
        dk_acc[...] = jnp.zeros_like(dk_acc)
        dv_acc[...] = jnp.zeros_like(dv_acc)
        keys = kv_ref[:, :HD].astype(jnp.float32)
        kr_ref[...] = rotate(keys, cos_ref[...], sin_ref[...]).astype(kr_ref.dtype)

    for step in range(rows // tile):
        here = pl.ds(step * tile, tile)
        width = (step + 1) * tile
        cosine, sine = cos_ref[here, :], sin_ref[here, :]
        query = rotate(q_ref[here, :].astype(jnp.float32), cosine, sine).astype(jnp.bfloat16)
        grad = g_ref[here, :].astype(jnp.bfloat16)
        keys = kr_ref[:width, :]
        values = kv_ref[:width, HD:]
        scores = dot(query, keys, 1, 1) * scale
        at_row = lax.broadcasted_iota(jnp.int32, scores.shape, 0) + step * tile
        at_col = lax.broadcasted_iota(jnp.int32, scores.shape, 1)
        allowed = (seg_col[here, :] == seg_row[:, :width]) & (at_col <= at_row)
        scores = jnp.where(allowed, scores, masked_score)
        weights = jnp.exp(scores - jnp.max(scores, axis=-1, keepdims=True))
        probs = weights * (1.0 / jnp.sum(weights, axis=-1, keepdims=True))
        probs_low = probs.astype(jnp.bfloat16)
        outputs = dot(probs_low, values, 1, 0).astype(jnp.bfloat16)
        o_ref[here, :] = outputs
        delta = jnp.sum(
            grad.astype(jnp.float32) * outputs.astype(jnp.float32), axis=-1, keepdims=True
        )
        dscore = (probs * (dot(grad, values, 1, 1) - delta)).astype(jnp.bfloat16)
        dquery = dot(dscore, keys, 1, 0) * scale
        dq_ref[here, :] = rotate(dquery, cosine, -sine).astype(dq_ref.dtype)
        dk_acc[:width, :] += dot(dscore, query, 0, 0) * scale
        dv_acc[:width, :] += dot(probs_low, grad, 0, 0)

    @pl.when(head == pl.num_programs(0) - 1)
    def _():
        dkv_ref[:, :HD] = rotate(dk_acc[...], cos_ref[...], -sin_ref[...]).astype(dkv_ref.dtype)
        dkv_ref[:, HD:] = dv_acc[...].astype(dkv_ref.dtype)


def attend(query, grad, kv, cosine, sine, segments):
    rows, columns = query.shape
    heads = columns // HD
    head_spec = pl.BlockSpec((rows, HD), lambda h: (0, h))

    def whole(shape):
        return pl.BlockSpec(shape, lambda h: (0, 0))

    return pl.pallas_call(
        functools.partial(attend_kernel, tile=min(256, rows)),
        grid=(heads,),
        out_shape=(
            jax.ShapeDtypeStruct((rows, columns), jnp.bfloat16),
            jax.ShapeDtypeStruct((rows, columns), jnp.bfloat16),
            jax.ShapeDtypeStruct((rows, 2 * HD), jnp.bfloat16),
        ),
        in_specs=[
            head_spec,
            head_spec,
            whole((rows, 2 * HD)),
            whole((rows, HD)),
            whole((rows, HD)),
            whole((rows, 1)),
            whole((1, rows)),
        ],
        out_specs=(head_spec, head_spec, whole((rows, 2 * HD))),
        scratch_shapes=[
            pltpu.VMEM((rows, HD), jnp.float32),
            pltpu.VMEM((rows, HD), jnp.float32),
            pltpu.VMEM((rows, HD), jnp.bfloat16),
        ],
        compiler_params=params(),
        cost_estimate=cost(10 * rows * rows * columns, 8 * 2**20),
    )(query, grad, kv, cosine, sine, segments[:, None], segments[None, :])


def input_grad_kernel(dq_ref, dkv_ref, wq_ref, wk_ref, wv_ref, o_ref):
    across, _, columns = dq_ref.shape
    total = None
    for m in range(across):
        term = dot(dq_ref[m], wq_ref[:, m * columns : (m + 1) * columns], 1, 1)
        total = term if total is None else total + term
    for g in range(dkv_ref.shape[0]):
        both = dkv_ref[g]
        total = total + dot(both[:, :HD], wk_ref[:, g * HD : (g + 1) * HD], 1, 1)
        total = total + dot(both[:, HD:], wv_ref[:, g * HD : (g + 1) * HD], 1, 1)
    o_ref[...] = total.astype(o_ref.dtype)


def input_grad_part(dq, dkv, wq, wk, wv):
    across, tokens, columns = dq.shape
    groups = dkv.shape[0]
    breadth = wq.shape[0]
    tile = min(256, tokens)

    def whole(x):
        return pl.BlockSpec(x.shape, lambda t: (0, 0))

    return pl.pallas_call(
        input_grad_kernel,
        grid=(tokens // tile,),
        out_shape=jax.ShapeDtypeStruct((tokens, breadth), jnp.bfloat16),
        in_specs=[
            pl.BlockSpec((across, tile, columns), lambda t: (0, t, 0)),
            pl.BlockSpec((groups, tile, 2 * HD), lambda t: (0, t, 0)),
            whole(wq),
            whole(wk),
            whole(wv),
        ],
        out_specs=pl.BlockSpec((tile, breadth), lambda t: (t, 0)),
        compiler_params=params(),
        cost_estimate=cost(2 * tokens * breadth * (columns * across + 2 * HD * groups), 2**24),
    )(dq, dkv, wq, wk, wv)


def qkv_grad_kernel(x_ref, dq_ref, dkv_ref, q_out, k_out, v_out, xt_ref):
    m = pl.program_id(0)

    @pl.when(m == 0)
    def _():
        xt_ref[...] = x_ref[...].T
        for g in range(dkv_ref.shape[0]):
            both = dot(xt_ref[...], dkv_ref[g], 1, 0).astype(k_out.dtype)
            k_out[:, g * HD : (g + 1) * HD] = both[:, :HD]
            v_out[:, g * HD : (g + 1) * HD] = both[:, HD:]

    q_out[...] = dot(xt_ref[...], dq_ref[0], 1, 0).astype(q_out.dtype)


def qkv_grads(x, dq, dkv):
    across, tokens, columns = dq.shape
    groups = dkv.shape[0]
    breadth = x.shape[1]
    return pl.pallas_call(
        qkv_grad_kernel,
        grid=(across,),
        out_shape=(
            jax.ShapeDtypeStruct((breadth, across * columns), jnp.bfloat16),
            jax.ShapeDtypeStruct((breadth, groups * HD), jnp.bfloat16),
            jax.ShapeDtypeStruct((breadth, groups * HD), jnp.bfloat16),
        ),
        in_specs=[
            pl.BlockSpec(x.shape, lambda m: (0, 0)),
            pl.BlockSpec((1, tokens, columns), lambda m: (m, 0, 0)),
            pl.BlockSpec(dkv.shape, lambda m: (0, 0, 0)),
        ],
        out_specs=(
            pl.BlockSpec((breadth, columns), lambda m: (0, m)),
            pl.BlockSpec((breadth, groups * HD), lambda m: (0, 0)),
            pl.BlockSpec((breadth, groups * HD), lambda m: (0, 0)),
        ),
        scratch_shapes=[pltpu.VMEM((breadth, tokens), jnp.bfloat16)],
        compiler_params=params(),
        cost_estimate=cost(2 * tokens * breadth * (columns * across + 2 * HD * groups), 2**24),
    )(x, dq, dkv)


def out_grad_kernel(a_ref, g_ref, o_ref):
    o_ref[...] = dot(a_ref[0].T, g_ref[...], 1, 0).astype(o_ref.dtype)


def out_grad(outputs, grad_out):
    across, tokens, columns = outputs.shape
    breadth = grad_out.shape[1]
    return pl.pallas_call(
        out_grad_kernel,
        grid=(across,),
        out_shape=jax.ShapeDtypeStruct((across * columns, breadth), jnp.bfloat16),
        in_specs=[
            pl.BlockSpec((1, tokens, columns), lambda m: (m, 0, 0)),
            pl.BlockSpec(grad_out.shape, lambda m: (0, 0)),
        ],
        out_specs=pl.BlockSpec((columns, breadth), lambda m: (m, 0)),
        compiler_params=params(),
        cost_estimate=cost(2 * tokens * breadth * columns * across, 2**24),
    )(outputs, grad_out)


def scatter_sum(x):
    return lax.psum_scatter(x, GROUP, scatter_dimension=0, tiled=True)


def gather(x):
    return lax.all_gather(x, GROUP, axis=0, tiled=True)


def per_device(
    hidden_states,
    grad_out,
    query_weight,
    key_weight,
    value_weight,
    output_weight,
    segment_ids,
    positions,
):
    across = lax.axis_size("gx")
    depth_count = lax.axis_size("gz")
    token_count = hidden_states.shape[0]
    kv_groups = key_weight.shape[1] // HD
    sharers = across // kv_groups
    columns = query_weight.shape[1] // across

    kv_part = project_kv(hidden_states, key_weight, value_weight, sharers, depth_count)
    kv_piece = scatter_sum(kv_part)
    kv = lax.all_gather(
        kv_piece,
        "gx",
        axis=0,
        tiled=True,
        axis_index_groups=[
            [g * sharers + s for s in range(sharers)] for g in range(kv_groups)
        ],
    )
    query = scatter_sum(project(hidden_states, query_weight, across, False))
    grad_heads = scatter_sum(project(grad_out, output_weight, across, True))
    cosine, sine = rope_tables(positions, HD)
    outputs, dquery, dkv = attend(query, grad_heads, kv, cosine, sine, segment_ids)

    dkv_all = (
        gather(dkv)
        .reshape(kv_groups, sharers, token_count, 2 * HD)
        .astype(jnp.float32)
        .sum(axis=1)
        .astype(jnp.bfloat16)
    )
    dq_all = gather(dquery).reshape(across, token_count, columns)
    summed = input_grad_part(dq_all, dkv_all, query_weight, key_weight, value_weight)
    input_grad = lax.psum_scatter(summed, "gy", scatter_dimension=0, tiled=True)
    outputs_all = gather(outputs).reshape(across, token_count, columns)
    query_weight_grad, key_weight_grad, value_weight_grad = qkv_grads(
        hidden_states, dq_all, dkv_all
    )
    output_weight_grad = out_grad(outputs_all, grad_out)
    return (input_grad, query_weight_grad, key_weight_grad, value_weight_grad, output_weight_grad)


def solution(mesh):
    placed = (
        P(None, GROUP),
        P(None, GROUP),
        P(GROUP, "gy"),
        P(GROUP, "gy"),
        P(GROUP, "gy"),
        P("gy", GROUP),
        P("gz"),
        P("gz"),
    )
    return jax.shard_map(
        per_device,
        mesh=mesh,
        in_specs=placed,
        out_specs=(
            P("gy", GROUP),
            P(GROUP, "gy"),
            P(GROUP, "gy"),
            P(GROUP, "gy"),
            P("gy", GROUP),
        ),
        check_vma=False,
    )
```

time: 663 us -> 469 us (0.71)
  waiting for transfers between devices: 172 us -> 321 us
  local copies, waits for them, and re-layouts: 143 us -> 1.65 us
  matrix products: 133 us -> 0 us
  blocking collectives: 131 us -> 4.01 us
  Pallas kernels: 0 us -> 119 us
  other arithmetic: 60.5 us -> 8.05 us
    psum x1 -> x0, blocking collectives: 131 us -> none  [per_device(): key_all, value_all = lax.psum((key_partial, value_partial), ('gx', 'gz'))]
    reduce_scatter x3 -> x4, waiting for transfers between devices: 67.7 us -> 194 us  [the longest x3 144 us: scatter_sum(): return lax.psum_scatter(x, GROUP, scatter_dimension=0, tiled=True)]
    dot_general x16 -> x0, matrix products: 122 us -> none  [the longest x1 16.4 us: per_device(): jnp.einsum('bta,abc->btc', source_rows, weight_cols, preferred_element_ty...]
    pallas_call x0 -> x7, Pallas kernels: none -> 119 us  [the longest x2 41.2 us: project(): pl.pallas_call(functools.partial(project_kernel, contract=1 if transposed...]
    gather x8 -> x0, local copies, waits for them, and re-layouts: 45.7 us -> none  [the longest x3 15.5 us: per_device(): source_rows = jnp.take(hidden_blocks, chosen % depth_count, axis=0)]
    all_gather x4 -> x3, waiting for transfers between devices: 82 us -> 126 us  [gather(): return lax.all_gather(x, GROUP, axis=0, tiled=True)]
    reshape x3 -> x0, local copies, waits for them, and re-layouts: 31.7 us -> none  [the longest x1 14.7 us: per_device(): key_each.reshape(kv_groups, sharers, token_count, heads_here, head_size)]
    unnamed x24 -> x4, local copies, waits for them, and re-layouts: 23.2 us -> 0.62 us
  transfers between devices with their start and end apart: 8 -> 7, of which waited for: 6 -> 6; matrix products, arithmetic and copies ran while one was open for 45% -> 2% of each run, Pallas kernels for 0% -> 19%
where the time goes in v1:
time: 469 us; the launch traced here: 468 us
  waiting for transfers between devices  321 us (68%)
  Pallas kernels  119 us (25%)
  between operations  14.1 us (3%)
  other arithmetic  8.05 us (2%)
    reduce_scatter x3, waiting for transfers between devices, scatter_sum(): return lax.psum_scatter(x, GROUP, scatter_dimension=0, tiled=True)  144 us
    all_gather x3, waiting for transfers between devices, gather(): return lax.all_gather(x, GROUP, axis=0, tiled=True)  126 us
    reduce_scatter x1, waiting for transfers between devices, per_device(): input_grad = lax.psum_scatter(summed, 'gy', scatter_dimension=0, tiled=True)  50.3 us
    pallas_call x2, Pallas kernels, project(): pl.pallas_call(functools.partial(project_kernel, contract=1 if transposed...  41.2 us
    pallas_call x1, Pallas kernels, attend(): pl.pallas_call(functools.partial(attend_kernel, tile=min(256, rows)), gri...  19.7 us
    pallas_call x1, Pallas kernels, input_grad_part(): pl.pallas_call(input_grad_kernel, grid=(tokens // tile,), out_shape=jax.S...  18.5 us
    pallas_call x1, Pallas kernels, qkv_grads(): pl.pallas_call(qkv_grad_kernel, grid=(across,), out_shape=(jax.ShapeDtype...  16.1 us
    pallas_call x1, Pallas kernels, out_grad(): pl.pallas_call(out_grad_kernel, grid=(across,), out_shape=jax.ShapeDtypeS...  13.3 us
  transfers between devices with their start and end apart: 7, of which 6 were waited for; matrix products, arithmetic and copies ran while one was open for 2% of the time, Pallas kernels for 19%

profile of v1, /device:TPU:0, one launch (start us, length us, event | category | flops | bytes accessed | tf_op | source)
XLA Modules:
  0.0 468.2 jit_solution(12310438784414819964)
XLA Ops:
  7.2 0.0 reduce-scatter.9.cloned.1.call-start
  7.2 9.9 %shard_map.121 = bf16[4096,256]{1,0:T(8,128)(2,1)} custom-call(bf16[2048,1024]{1,0:T(8,128)(2,1)} %x_ref.7, bf16[1024,256]{1,0:T(8,128)(2,1)} %wk_ref.1, bf16[1024,256]{1,0:T(8,128)(2,1)} %wv_ref.1), custom_call_target="tpu_custom_call" | custom-call | flops 2147483648 | bytes 8388608 | tf_op jit(solution)/shard_map/pallas_call | solution.py:78
  17.2 0.0 reduce-scatter.9.cloned.1.call-update
  17.2 0.0 reduce-scatter.5.cloned.1.call-start
  17.2 20.6 %shard_map.119 = bf16[8192,512]{1,0:T(8,128)(2,1)} custom-call(bf16[2048,1024]{1,0:T(8,128)(2,1)} %x_ref.7, bf16[1024,2048]{1,0:T(8,128)(2,1)} %wq_ref.1), custom_call_target="tpu_custom_call" | custom-call | flops 8589934592 | bytes 16777216 | tf_op jit(solution)/shard_map/pallas_call | solution.py:56
  37.9 0.0 reduce-scatter.5.cloned.1.call-update
  37.9 0.0 reduce-scatter.7.cloned.1.call-start
  37.9 20.6 %shard_map.120 = bf16[8192,512]{1,0:T(8,128)(2,1)} custom-call(bf16[2048,1024]{1,0:T(8,128)(2,1)} %g_ref.1, bf16[2048,1024]{1,0:T(8,128)(2,1)} %w_ref.3), custom_call_target="tpu_custom_call" | custom-call | flops 8589934592 | bytes 16777216 | tf_op jit(solution)/shard_map/pallas_call | solution.py:56
  58.6 0.0 all-gather.6.cloned.1.call-start
  58.6 0.6 copy-done.1
  59.2 1.0 copy.13.seg_col
  60.3 1.9 fusion
  62.2 1.3 pad_maximum_fusion
  63.5 4.0 all_gather.12.kv_ref
  67.5 68.9 %reduce-scatter.5.cloned.1.call-done.q_ref = bf16[1024,512]{1,0:T(8,128)(2,1)} async-done(((bf16[8192,512]{1,0:T(8,128)(2,1)}), bf16[1024,512]{1,0:T(8,128)(2,1)}) %reduce-scatter.5.cloned.1.call-update) | async-done | bytes 1048592 | tf_op jit(solution)/shard_map/reduce_scatter | solution.py:281
  136.4 74.8 %reduce-scatter.7.cloned.1.call-done.g_ref = bf16[1024,512]{1,0:T(8,128)(2,1)} async-done(((bf16[8192,512]{1,0:T(8,128)(2,1)}), bf16[1024,512]{1,0:T(8,128)(2,1)}) %reduce-scatter.7.cloned.1.call-update) | async-done | bytes 1048592 | tf_op jit(solution)/shard_map/reduce_scatter | solution.py:281
  211.2 19.7 %shard_map.122 = (bf16[1024,512]{1,0:T(8,128)(2,1)}, bf16[1024,512]{1,0:T(8,128)(2,1)}, bf16[1024,256]{1,0:T(8,128)(2,1)}) custom-call(bf16[1024,512]{1,0:T(8,128)(2,1)} %reduce-scatter.5.cloned.1.call-done.q_ref, bf16[1024,512]{1,0:T(8,128)(2,1)} %reduce-scatter.7.cloned.1.call-done.g_ref, bf16[1024,256]{1,0:T(8,128)(2,1)} %all_gather.12.kv_ref, ...), custom_call_target="tpu_custom_call" | custom-call | flops 5368709120 | bytes 8388608 | tf_op jit(solution)/shard_map/pallas_call | solution.py:150
  230.9 0.0 all-gather.6.cloned.1.call-update
  230.9 0.0 all-gather.4.cloned.1.call-start
  231.0 0.5 all-gather.4.cloned.1.call-update
  231.5 0.0 all-gather.8.cloned.1.call-start
  231.6 0.5 all-gather.8.cloned.1.call-update
  232.1 0.2 reduce-scatter.11.cloned.1.call-start
  232.3 35.5 %all-gather.6.cloned.1.call-done = bf16[8192,256]{1,0:T(8,128)(2,1)} async-done(((bf16[1024,256]{1,0:T(8,128)(2,1)}), bf16[8192,256]{1,0:T(8,128)(2,1)}) %all-gather.6.cloned.1.call-update) | async-done | bytes 4194320 | tf_op jit(solution)/shard_map/all_gather | solution.py:285
  267.8 4.8 %reduce_sum.12.dkv_ref = bf16[2,2048,256]{2,1,0:T(8,128)(2,1)} reduce(bf16[2,2,2048,256]{3,2,1,0:T(8,128)(2,1)} %bitcast.5, bf16[]{:T(256)} %constant.9.clone.1), dimensions={1}, to_apply=%region_3.0 | reduce | flops 1048576 | bytes 6291458 | tf_op jit(solution)/shard_map/reduce_sum | solution.py:325
  272.6 52.1 %all-gather.4.cloned.1.call-done = bf16[8192,512]{1,0:T(8,128)(2,1)} async-done(((bf16[1024,512]{1,0:T(8,128)(2,1)}), bf16[8192,512]{1,0:T(8,128)(2,1)}) %all-gather.4.cloned.1.call-update) | async-done | bytes 8388624 | tf_op jit(solution)/shard_map/all_gather | solution.py:285
  324.7 18.5 %shard_map.123 = bf16[2048,1024]{1,0:T(8,128)(2,1)} custom-call(bf16[4,2048,512]{2,1,0:T(8,128)(2,1)} %bitcast.8, bf16[2,2048,256]{2,1,0:T(8,128)(2,1)} %reduce_sum.12.dkv_ref, bf16[1024,2048]{1,0:T(8,128)(2,1)} %wq_ref.1, bf16[1024,256]{1,0:T(8,128)(2,1)} %wk_ref.1, bf16[1024,256]{1,0:T(8,128)(2,1)} %wv_ref.1), custom_call_target="tpu_custom_call" | custom-call | flops 10737418240 | bytes 16777216 | tf_op jit(solution)/shard_map/pallas_call | solution.py:200
  343.1 0.0 reduce-scatter.11.cloned.1.call-update
  343.2 38.5 %all-gather.8.cloned.1.call-done = bf16[8192,512]{1,0:T(8,128)(2,1)} async-done(((bf16[1024,512]{1,0:T(8,128)(2,1)}), bf16[8192,512]{1,0:T(8,128)(2,1)}) %all-gather.8.cloned.1.call-update) | async-done | bytes 8388624 | tf_op jit(solution)/shard_map/all_gather | solution.py:285
  381.6 13.3 %shard_map.125 = bf16[2048,1024]{1,0:T(8,128)(2,1)} custom-call(bf16[4,2048,512]{2,1,0:T(8,128)(2,1)} %bitcast.10, bf16[2048,1024]{1,0:T(8,128)(2,1)} %g_ref.1), custom_call_target="tpu_custom_call" | custom-call | flops 8589934592 | bytes 16777216 | tf_op jit(solution)/shard_map/pallas_call | solution.py:266
  394.9 16.1 %shard_map.124 = (bf16[1024,2048]{1,0:T(8,128)(2,1)}, bf16[1024,256]{1,0:T(8,128)(2,1)}, bf16[1024,256]{1,0:T(8,128)(2,1)}) custom-call(bf16[2048,1024]{1,0:T(8,128)(2,1)} %x_ref.7, bf16[4,2048,512]{2,1,0:T(8,128)(2,1)} %bitcast.9, bf16[2,2048,256]{2,1,0:T(8,128)(2,1)} %reduce_sum.12.dkv_ref), custom_call_target="tpu_custom_call" | custom-call | flops 10737418240 | bytes 16777216 | tf_op jit(solution)/shard_map/pallas_call | solution.py:235
  411.1 50.3 %reduce-scatter.11.cloned.1.call-done = bf16[512,1024]{1,0:T(8,128)(2,1)} async-done(((bf16[2048,1024]{1,0:T(8,128)(2,1)}), bf16[512,1024]{1,0:T(8,128)(2,1)}) %reduce-scatter.11.cloned.1.call-update) | async-done | bytes 1048592 | tf_op jit(solution)/shard_map/reduce_scatter | solution.py:330
  (7 shorter events, 0.0 us)
Async XLA Ops:
  7.2 56.3 %reduce-scatter.9.cloned.1.call-start = ((), (), s32[]{:S(2)}) async-start(), calls=%async_computation.6 | async-start | bytes 2359296 | tf_op jit(solution)/shard_map/reduce_scatter | solution.py:281
  17.2 119.3 %reduce-scatter.5.cloned.1.call-start = ((), (), s32[]{:S(2)}) async-start(), calls=%async_computation.4 | async-start | bytes 9437184 | tf_op jit(solution)/shard_map/reduce_scatter | solution.py:281
  37.9 173.3 %reduce-scatter.7.cloned.1.call-start = ((), (), s32[]{:S(2)}) async-start(), calls=%async_computation.5 | async-start | bytes 9437184 | tf_op jit(solution)/shard_map/reduce_scatter | solution.py:281
  58.5 0.7 copy-start.1
  58.5 0.7 copy-start
  58.6 209.2 %all-gather.6.cloned.1.call-start = ((), (), s32[]{:S(2)}) async-start(), calls=%async_computation.8 | async-start | bytes 4718592 | tf_op jit(solution)/shard_map/all_gather | solution.py:285
  230.9 93.7 %all-gather.4.cloned.1.call-start = ((), (), s32[]{:S(2)}) async-start(), calls=%async_computation.7 | async-start | bytes 9437184 | tf_op jit(solution)/shard_map/all_gather | solution.py:285
  231.5 150.1 %all-gather.8.cloned.1.call-start = ((), (), s32[]{:S(2)}) async-start(), calls=%async_computation.10 | async-start | bytes 9437184 | tf_op jit(solution)/shard_map/all_gather | solution.py:285
  232.1 229.3 %reduce-scatter.11.cloned.1.call-start = ((), (), s32[]{:S(2)}) async-start(), calls=%async_computation.9 | async-start | bytes 5242880 | tf_op jit(solution)/shard_map/reduce_scatter | solution.py:330
Sparse Core Ops, SparseCore 0:
  17.3 43.9 reduce-scatter.8
  65.1 71.2 reduce-scatter.4
  139.9 71.2 reduce-scatter.6
  231.1 36.6 all-gather.5
  270.3 54.3 all-gather.3
  327.1 54.4 all-gather.7
  384.6 76.7 reduce-scatter.10

commit v2 on v1

--- a/solution.py
+++ b/solution.py
@@ -10,6 +10,7 @@
 
 HD = 128
 GROUP = ("gx", "gz")
+MESH = pl.DeviceIdType.MESH
 
 rope_base = 10000.0
 masked_score = -1e30
@@ -40,56 +41,290 @@
     return values * cosine + pltpu.roll(values, values.shape[-1] // 2, 1) * sine
 
 
-def project_kernel(x_ref, w_ref, o_ref, *, contract):
-    o_ref[...] = dot(x_ref[...], w_ref[...], 1, contract).astype(o_ref.dtype)
-
-
-def project(x, weight, across, transposed):
-    tokens, depth = x.shape
-    columns = weight.shape[0 if transposed else 1] // across
-    tile = min(512, tokens)
-    steps = tokens // tile
-    if transposed:
-        w_spec = pl.BlockSpec((columns, depth), lambda m, t: (m, 0))
-    else:
-        w_spec = pl.BlockSpec((depth, columns), lambda m, t: (0, m))
+class Place:
+    def __init__(self, across, depth_count):
+        self.chips, self.depth = across // 2, depth_count
+        self.count = self.chips * depth_count
+        member = lax.axis_index("gx")
+        self.chip, self.core = member // 2, member % 2
+        self.z = lax.axis_index("gz")
+
+    def ahead(self, offset):
+        return (
+            lax.rem(self.chip + offset // self.depth, self.chips),
+            lax.rem(self.z + offset % self.depth, self.depth),
+        )
+
+    def behind(self, offset):
+        return (
+            lax.rem(self.chip + self.chips - offset // self.depth, self.chips),
+            lax.rem(self.z + self.depth - offset % self.depth, self.depth),
+        )
+
+    def device(self, chip, z, core):
+        return {"gx": chip * 2 + core, "gz": z}
+
+    def partner(self):
+        return self.device(self.chip, self.z, 1 - self.core)
+
+    def meet(self):
+        barrier = pltpu.get_barrier_semaphore()
+        pl.semaphore_signal(barrier, inc=1, device_id=self.partner(), device_id_type=MESH)
+        for offset in range(1, self.count):
+            chip, z = self.ahead(offset)
+            pl.semaphore_signal(
+                barrier, inc=1, device_id=self.device(chip, z, self.core), device_id_type=MESH
+            )
+        pl.semaphore_wait(barrier, self.count)
+
+
+def send(src, dst, send_sem, recv_sem, device):
+    return pltpu.make_async_remote_copy(
+        src_ref=src,
+        dst_ref=dst,
+        send_sem=send_sem,
+        recv_sem=recv_sem,
+        device_id=device,
+        device_id_type=MESH,
+    )
+
+
+def project_sum_kernel(
+    x_ref, y_ref, wq_ref, wk_ref, wv_ref, wo_ref, q_out, g_out, kv_out,
+    kv_give, kv_take, kv_mine, kv_land, kv_half, kv_other,
+    q_give, q_take, q_mine, q_land,
+    g_give, g_take, g_mine, g_land,
+    pair_send, pair_recv, chip_send, chip_recv, half_send, half_recv,
+    *, across, depth_count, sharers,
+):
+    at = Place(across, depth_count)
+    block, columns = q_out.shape
+    half = block // 2
+    dtype = q_out.dtype
+    tile = min(256, half)
+    at.meet()
+    give, take = (kv_give, q_give, g_give), (kv_take, q_take, g_take)
+    mine, land = (kv_mine, q_mine, g_mine), (kv_land, q_land, g_land)
+
+    def compute(which, offset):
+        chip, z = at.ahead(offset)
+
+        def rows(start, i):
+            return pl.ds(pl.multiple_of(start + i * tile, tile), tile)
+
+        def body(i, carry):
+            here = pl.ds(pl.multiple_of(i * tile, tile), tile)
+            for core, into in ((1 - at.core, give[which]), (at.core, mine[which])):
+                if which == 0:
+                    head = (2 * chip) // sharers
+                    cols = pl.ds(pl.multiple_of(head * HD, HD), HD)
+                    x = x_ref[rows(z * block + core * half, i), :]
+                    into[offset, here, :HD] = dot(x, wk_ref[:, cols], 1, 0).astype(dtype)
+                    into[offset, here, HD:] = dot(x, wv_ref[:, cols], 1, 0).astype(dtype)
+                else:
+                    cols = pl.ds(pl.multiple_of((chip * 2 + core) * columns, HD), columns)
+                    if which == 1:
+                        term = dot(x_ref[rows(z * block, i), :], wq_ref[:, cols], 1, 0)
+                    else:
+                        term = dot(y_ref[rows(z * block, i), :], wo_ref[cols, :], 1, 1)
+                    into[offset, here, :] = term.astype(dtype)
+            return carry
+
+        lax.fori_loop(0, mine[which].shape[1] // tile, body, 0)
+        copy = send(
+            give[which].at[offset],
+            take[which].at[offset],
+            pair_send.at[which, offset],
+            pair_recv.at[which, offset],
+            at.partner(),
+        )
+        copy.start()
+        return copy
+
+    def forward(which, offset, pair_copy):
+        pair_copy.wait_recv()
+
+        def body(i, carry):
+            here = pl.ds(pl.multiple_of(i * tile, tile), tile)
+            total = mine[which][offset, here, :].astype(jnp.float32) + take[which][
+                offset, here, :
+            ].astype(jnp.float32)
+            mine[which][offset, here, :] = total.astype(dtype)
+            return carry
+
+        lax.fori_loop(0, mine[which].shape[1] // tile, body, 0)
+        if offset == 0:
+            return None
+        chip, z = at.ahead(offset)
+        copy = send(
+            mine[which].at[offset],
+            land[which].at[offset - 1],
+            chip_send.at[which, offset],
+            chip_recv.at[which, offset],
+            at.device(chip, z, at.core),
+        )
+        copy.start()
+        return copy
+
+    def finish(which, out):
+        def body(i, carry):
+            here = pl.ds(pl.multiple_of(i * tile, tile), tile)
+            total = mine[which][0, here, :].astype(jnp.float32)
+            for other in range(at.count - 1):
+                total = total + land[which][other, here, :].astype(jnp.float32)
+            out[here, :] = total.astype(dtype)
+            return carry
+
+        lax.fori_loop(0, mine[which].shape[1] // tile, body, 0)
+
+    offsets = list(range(1, at.count)) + [0]
+    steps = [(which, offset) for which in range(3) for offset in offsets]
+    pairs, chips = [], [[], [], []]
+    for which, offset in steps:
+        pairs.append(compute(which, offset))
+        done = len(pairs) - 2
+        if done >= 0:
+            before, place = steps[done]
+            chips[before].append(forward(before, place, pairs[done]))
+    chips[2].append(forward(2, 0, pairs[-1]))
+
+    for copy in chips[0][:-1]:
+        copy.wait_recv()
+    finish(0, kv_half)
+    swap = send(kv_half, kv_other, half_send, half_recv, at.partner())
+    swap.start()
+    for copy in chips[1][:-1]:
+        copy.wait_recv()
+    finish(1, q_out)
+    swap.wait()
+    kv_out[pl.ds(pl.multiple_of(at.core * half, half), half), :] = kv_half[...]
+    kv_out[pl.ds(pl.multiple_of((1 - at.core) * half, half), half), :] = kv_other[...]
+    for copy in chips[2][:-1]:
+        copy.wait_recv()
+    finish(2, g_out)
+    for copy in pairs:
+        copy.wait_send()
+    for group in chips:
+        for copy in group[:-1]:
+            copy.wait_send()
+
+
+def project_sum(x, y, wq, wk, wv, wo, across, depth_count, sharers):
+    tokens = x.shape[0]
+    block, columns = tokens // depth_count, wq.shape[1] // across
+    half, count = block // 2, across // 2 * depth_count
+    low = jnp.bfloat16
+
+    def slots(number, rows, width):
+        return pltpu.VMEM((number, rows, width), low)
+
+    def buffers(rows, width):
+        return [slots(count, rows, width)] * 3 + [slots(count - 1, rows, width)]
+
+    dma = pltpu.SemaphoreType.DMA
     return pl.pallas_call(
-        functools.partial(project_kernel, contract=1 if transposed else 0),
-        grid=(across, steps),
-        out_shape=jax.ShapeDtypeStruct((across * tokens, columns), jnp.bfloat16),
-        in_specs=[pl.BlockSpec((tile, depth), lambda m, t: (t, 0)), w_spec],
-        out_specs=pl.BlockSpec((tile, columns), lambda m, t: (m * steps + t, 0)),
-        compiler_params=params(),
-        cost_estimate=cost(2 * tokens * depth * columns * across, 16 * 2**20),
-    )(x, weight)
-
-
-def project_kv_kernel(x_ref, k_ref, v_ref, o_ref):
-    x = x_ref[...]
-    o_ref[:, :HD] = dot(x, k_ref[...], 1, 0).astype(o_ref.dtype)
-    o_ref[:, HD:] = dot(x, v_ref[...], 1, 0).astype(o_ref.dtype)
-
-
-def project_kv(x, key_weight, value_weight, sharers, depth_count):
-    tokens, depth = x.shape
-    kv_groups = key_weight.shape[1] // HD
-    rows = tokens // depth_count // sharers
-    w_spec = pl.BlockSpec((depth, HD), lambda g, s, z: (0, g))
+        functools.partial(
+            project_sum_kernel, across=across, depth_count=depth_count, sharers=sharers
+        ),
+        out_shape=(
+            jax.ShapeDtypeStruct((block, columns), low),
+            jax.ShapeDtypeStruct((block, columns), low),
+            jax.ShapeDtypeStruct((block, 2 * HD), low),
+        ),
+        in_specs=[pl.BlockSpec(memory_space=pltpu.VMEM)] * 6,
+        out_specs=(pl.BlockSpec(memory_space=pltpu.VMEM),) * 3,
+        scratch_shapes=buffers(half, 2 * HD)
+        + [pltpu.VMEM((half, 2 * HD), low)] * 2
+        + buffers(block, columns)
+        + buffers(block, columns)
+        + [dma((3, count))] * 4
+        + [dma, dma],
+        compiler_params=pltpu.CompilerParams(
+            vmem_limit_bytes=60 * 1024 * 1024, collective_id=0, has_side_effects=True
+        ),
+        cost_estimate=cost(4 * tokens * x.shape[1] * columns * across, 2**25),
+    )(x, y, wq, wk, wv, wo)
+
+
+def gather_kernel(*refs, number, across, depth_count):
+    ins, outs = refs[:number], refs[number : 2 * number]
+    chip_send, chip_recv, pair_send, pair_recv, own_sem = refs[2 * number :]
+    at = Place(across, depth_count)
+    member = at.chip * 2 + at.core
+    at.meet()
+    sends, chips, pairs, owns = [], {}, [], []
+    for i in range(number):
+        for offset in range(1, at.count):
+            chip, z = at.ahead(offset)
+            copy = send(
+                ins[i],
+                outs[i].at[member, at.z],
+                chip_send.at[i, offset],
+                chip_recv.at[i, offset],
+                at.device(chip, z, at.core),
+            )
+            copy.start()
+            sends.append(copy)
+        copy = send(
+            ins[i],
+            outs[i].at[member, at.z],
+            pair_send.at[i, 0],
+            pair_recv.at[i, 0],
+            at.partner(),
+        )
+        copy.start()
+        pairs.append((i, 0, copy))
+        own = pltpu.make_async_copy(ins[i], outs[i].at[member, at.z], own_sem.at[i])
+        own.start()
+        owns.append(own)
+    for i in range(number):
+        for offset in range(1, at.count):
+            chip, z = at.behind(offset)
+            arrived = outs[i].at[chip * 2 + at.core, z]
+            send(
+                ins[i],
+                arrived,
+                chip_send.at[i, offset],
+                chip_recv.at[i, offset],
+                at.device(chip, z, at.core),
+            ).wait_recv()
+            copy = send(
+                arrived, arrived, pair_send.at[i, offset], pair_recv.at[i, offset], at.partner()
+            )
+            copy.start()
+            pairs.append((i, offset, copy))
+    for own in owns:
+        own.wait()
+    for copy in sends:
+        copy.wait_send()
+    for i, offset, copy in pairs:
+        copy.wait_send()
+        chip, z = at.behind(offset)
+        send(
+            ins[i],
+            outs[i].at[chip * 2 + 1 - at.core, z],
+            pair_send.at[i, offset],
+            pair_recv.at[i, offset],
+            at.partner(),
+        ).wait_recv()
+
+
+def gather(arrays, across, depth_count, collective_id):
+    number, count = len(arrays), across // 2 * depth_count
+    dma = pltpu.SemaphoreType.DMA
     return pl.pallas_call(
-        project_kv_kernel,
-        grid=(kv_groups, sharers, depth_count),
-        out_shape=jax.ShapeDtypeStruct((kv_groups * tokens, 2 * HD), jnp.bfloat16),
-        in_specs=[
-            pl.BlockSpec((rows, depth), lambda g, s, z: (z * sharers + s, 0)),
-            w_spec,
-            w_spec,
-        ],
-        out_specs=pl.BlockSpec(
-            (rows, 2 * HD), lambda g, s, z: ((g * sharers + s) * depth_count + z, 0)
-        ),
-        compiler_params=params(),
-        cost_estimate=cost(4 * tokens * depth * HD * kv_groups, 8 * 2**20),
-    )(x, key_weight, value_weight)
+        functools.partial(gather_kernel, number=number, across=across, depth_count=depth_count),
+        out_shape=tuple(
+            jax.ShapeDtypeStruct((across, depth_count) + x.shape, x.dtype) for x in arrays
+        ),
+        in_specs=[pl.BlockSpec(memory_space=pl.ANY)] * number,
+        out_specs=(pl.BlockSpec(memory_space=pl.ANY),) * number,
+        scratch_shapes=[dma((number, count))] * 4 + [dma((number,))],
+        compiler_params=pltpu.CompilerParams(
+            vmem_limit_bytes=VMEM_LIMIT, collective_id=collective_id, has_side_effects=True
+        ),
+        cost_estimate=cost(0, 2**27),
+    )(*arrays)
 
 
 def attend_kernel(
@@ -277,14 +512,6 @@
     )(outputs, grad_out)
 
 
-def scatter_sum(x):
-    return lax.psum_scatter(x, GROUP, scatter_dimension=0, tiled=True)
-
-
-def gather(x):
-    return lax.all_gather(x, GROUP, axis=0, tiled=True)
-
-
 def per_device(
     hidden_states,
     grad_out,
@@ -302,33 +529,33 @@
     sharers = across // kv_groups
     columns = query_weight.shape[1] // across
 
-    kv_part = project_kv(hidden_states, key_weight, value_weight, sharers, depth_count)
-    kv_piece = scatter_sum(kv_part)
-    kv = lax.all_gather(
-        kv_piece,
-        "gx",
-        axis=0,
-        tiled=True,
-        axis_index_groups=[
-            [g * sharers + s for s in range(sharers)] for g in range(kv_groups)
-        ],
+    query, grad_heads, kv = project_sum(
+        hidden_states,
+        grad_out,
+        query_weight,
+        key_weight,
+        value_weight,
+        output_weight,
+        across,
+        depth_count,
+        sharers,
     )
-    query = scatter_sum(project(hidden_states, query_weight, across, False))
-    grad_heads = scatter_sum(project(grad_out, output_weight, across, True))
     cosine, sine = rope_tables(positions, HD)
     outputs, dquery, dkv = attend(query, grad_heads, kv, cosine, sine, segment_ids)
 
+    dkv_all, dq_all = gather((dkv, dquery), across, depth_count, 1)
     dkv_all = (
-        gather(dkv)
-        .reshape(kv_groups, sharers, token_count, 2 * HD)
+        dkv_all.reshape(kv_groups, sharers, token_count, 2 * HD)
         .astype(jnp.float32)
         .sum(axis=1)
         .astype(jnp.bfloat16)
     )
-    dq_all = gather(dquery).reshape(across, token_count, columns)
+    dq_all = dq_all.reshape(across, token_count, columns)
     summed = input_grad_part(dq_all, dkv_all, query_weight, key_weight, value_weight)
+    outputs, summed = lax.optimization_barrier((outputs, summed))
     input_grad = lax.psum_scatter(summed, "gy", scatter_dimension=0, tiled=True)
-    outputs_all = gather(outputs).reshape(across, token_count, columns)
+    (outputs_all,) = gather((outputs,), across, depth_count, 2)
+    outputs_all = outputs_all.reshape(across, token_count, columns)
     query_weight_grad, key_weight_grad, value_weight_grad = qkv_grads(
         hidden_states, dq_all, dkv_all
     )

time: 469 us -> 338 us (0.72)
  waiting for transfers between devices: 321 us -> 0.02 us
  Pallas kernels: 119 us -> 313 us
    pallas_call x3, Pallas kernels: 51.2 us -> 245 us  [the longest x2 126 us: gather(): pl.pallas_call(functools.partial(gather_kernel, number=number, across=acr...]
    reduce_scatter x3 -> x0, waiting for transfers between devices: 144 us -> none  [scatter_sum(): return lax.psum_scatter(x, GROUP, scatter_dimension=0, tiled=True)]
    all_gather x3 -> x0, waiting for transfers between devices: 126 us -> none  [gather(): return lax.all_gather(x, GROUP, axis=0, tiled=True)]
    reduce_scatter x1, waiting for transfers between devices: 50.3 us -> 0.01 us  [per_device(): input_grad = lax.psum_scatter(summed, 'gy', scatter_dimension=0, tiled=True)]
  transfers between devices with their start and end apart: 7 -> 1, of which waited for: 6 -> 0; matrix products, arithmetic and copies ran while one was open for 2% -> 0% of each run, Pallas kernels for 19% -> 24%
where the time goes in v2:
time: 338 us
  Pallas kernels  313 us (93%)
  between operations  14.1 us (4%)
  other arithmetic  8.72 us (3%)
    pallas_call x2, Pallas kernels, gather(): pl.pallas_call(functools.partial(gather_kernel, number=number, across=acr...  126 us
    pallas_call x1, Pallas kernels, project_sum(): pl.pallas_call(functools.partial(project_sum_kernel, across=across, depth...  120 us
    pallas_call x1, Pallas kernels, attend(): pl.pallas_call(functools.partial(attend_kernel, tile=min(256, rows)), gri...  19.8 us
    pallas_call x1, Pallas kernels, input_grad_part(): pl.pallas_call(input_grad_kernel, grid=(tokens // tile,), out_shape=jax.S...  18.4 us
    pallas_call x1, Pallas kernels, qkv_grads(): pl.pallas_call(qkv_grad_kernel, grid=(across,), out_shape=(jax.ShapeDtype...  16.2 us
    pallas_call x1, Pallas kernels, out_grad(): pl.pallas_call(out_grad_kernel, grid=(across,), out_shape=jax.ShapeDtypeS...  13.3 us
  transfers between devices with their start and end apart: 1, of which 0 were waited for; matrix products, arithmetic and copies ran while one was open for 0% of the time, Pallas kernels for 24%

profile of v2, /device:TPU:0, one launch (start us, length us, event | category | flops | bytes accessed | tf_op | source)
XLA Modules:
  0.0 337.8 jit_solution(14086368801098191064)
XLA Ops:
  7.2 0.0 reduce-scatter.2.cloned.1.call-start
  7.2 0.7 convert_element_type.2
  7.9 1.7 copy.13.seg_col
  9.6 1.9 fusion
  11.5 1.3 pad_maximum_fusion
  12.8 119.6 %shard_map.119 = (bf16[1024,512]{1,0:T(8,128)(2,1)}, bf16[1024,512]{1,0:T(8,128)(2,1)}, bf16[1024,256]{1,0:T(8,128)(2,1)}) custom-call(bf16[2048,1024]{1,0:T(8,128)(2,1)} %x_ref.3, bf16[2048,1024]{1,0:T(8,128)(2,1)} %g_ref.1, bf16[1024,2048]{1,0:T(8,128)(2,1)} %wq_ref.3, bf16[1024,256]{1,0:T(8,128)(2,1)} %wk_ref.3, bf16[1024,256]{1,0:T(8,128)(2,1)} %wv_ref.3, ...), custom_call_target="tpu_custom_call" | custom-call | flops 17179869184 | bytes 33554432 | tf_op jit(solution)/shard_map/pallas_call | solution.py:225
  132.4 19.8 %shard_map.120 = (bf16[1024,512]{1,0:T(8,128)(2,1)}, bf16[1024,512]{1,0:T(8,128)(2,1)}, bf16[1024,256]{1,0:T(8,128)(2,1)}) custom-call(bf16[1024,512]{1,0:T(8,128)(2,1)} %get-tuple-element.18.q_ref, bf16[1024,512]{1,0:T(8,128)(2,1)} %get-tuple-element.19.g_ref, bf16[1024,256]{1,0:T(8,128)(2,1)} %get-tuple-element.20.kv_ref, ...), custom_call_target="tpu_custom_call" | custom-call | flops 5368709120 | bytes 8388608 | tf_op jit(solution)/shard_map/pallas_call | solution.py:385
  152.2 73.9 %shard_map.121 = (bf16[4,2,1024,256]{3,2,1,0:T(8,128)(2,1)}, bf16[4,2,1024,512]{3,2,1,0:T(8,128)(2,1)}) custom-call(bf16[1024,256]{1,0:T(8,128)(2,1)} %get-tuple-element.22.refs_0_, bf16[1024,512]{1,0:T(8,128)(2,1)} %get-tuple-element.23.refs_1_), custom_call_target="tpu_custom_call" | custom-call | bytes 134217728 | tf_op jit(solution)/shard_map/pallas_call | solution.py:315
  226.1 4.8 %reduce_sum.12.dkv_ref = bf16[2,2048,256]{2,1,0:T(8,128)(2,1)} reduce(bf16[2,2,2048,256]{3,2,1,0:T(8,128)(2,1)} %bitcast.6, bf16[]{:T(256)} %constant.9.clone.1), dimensions={1}, to_apply=%region_0.0 | reduce | flops 1048576 | bytes 6291458 | tf_op jit(solution)/shard_map/reduce_sum | solution.py:550
  230.9 18.4 %shard_map.122 = bf16[2048,1024]{1,0:T(8,128)(2,1)} custom-call(bf16[4,2048,512]{2,1,0:T(8,128)(2,1)} %bitcast.9, bf16[2,2048,256]{2,1,0:T(8,128)(2,1)} %reduce_sum.12.dkv_ref, bf16[1024,2048]{1,0:T(8,128)(2,1)} %wq_ref.3, bf16[1024,256]{1,0:T(8,128)(2,1)} %wk_ref.3, bf16[1024,256]{1,0:T(8,128)(2,1)} %wv_ref.3), custom_call_target="tpu_custom_call" | custom-call | flops 10737418240 | bytes 16777216 | tf_op jit(solution)/shard_map/pallas_call | solution.py:435
  249.3 0.0 reduce-scatter.2.cloned.1.call-update
  249.4 52.0 %shard_map.124 = bf16[4,2,1024,512]{3,2,1,0:T(8,128)(2,1)} custom-call(bf16[1024,512]{1,0:T(8,128)(2,1)} %get-tuple-element.30.refs_0_), custom_call_target="tpu_custom_call" | custom-call | bytes 134217728 | tf_op jit(solution)/shard_map/pallas_call | solution.py:315
  301.4 13.3 %shard_map.125 = bf16[2048,1024]{1,0:T(8,128)(2,1)} custom-call(bf16[4,2048,512]{2,1,0:T(8,128)(2,1)} %bitcast.5, bf16[2048,1024]{1,0:T(8,128)(2,1)} %g_ref.1), custom_call_target="tpu_custom_call" | custom-call | flops 8589934592 | bytes 16777216 | tf_op jit(solution)/shard_map/pallas_call | solution.py:501
  314.7 16.2 %shard_map.123 = (bf16[1024,2048]{1,0:T(8,128)(2,1)}, bf16[1024,256]{1,0:T(8,128)(2,1)}, bf16[1024,256]{1,0:T(8,128)(2,1)}) custom-call(bf16[2048,1024]{1,0:T(8,128)(2,1)} %x_ref.3, bf16[4,2048,512]{2,1,0:T(8,128)(2,1)} %bitcast.10, bf16[2,2048,256]{2,1,0:T(8,128)(2,1)} %reduce_sum.12.dkv_ref), custom_call_target="tpu_custom_call" | custom-call | flops 10737418240 | bytes 16777216 | tf_op jit(solution)/shard_map/pallas_call | solution.py:470
  330.9 0.0 reduce-scatter.2.cloned.1.call-done
  (1 shorter events, 0.0 us)
Async XLA Ops:
  7.2 323.8 %reduce-scatter.2.cloned.1.call-start = ((), (), s32[]{:S(2)}) async-start(), calls=%async_computation.1 | async-start | bytes 5242880 | tf_op jit(solution)/shard_map/reduce_scatter | solution.py:556
Sparse Core Ops, SparseCore 0:
  249.5 77.3 reduce-scatter.1

commit v3 on v2

--- a/solution.py
+++ b/solution.py
@@ -45,6 +45,7 @@
     def __init__(self, across, depth_count):
         self.chips, self.depth = across // 2, depth_count
         self.count = self.chips * depth_count
+        self.square = self.chips == 2 and depth_count == 2
         member = lax.axis_index("gx")
         self.chip, self.core = member // 2, member % 2
         self.z = lax.axis_index("gz")
@@ -94,7 +95,7 @@
     kv_give, kv_take, kv_mine, kv_land, kv_half, kv_other,
     q_give, q_take, q_mine, q_land,
     g_give, g_take, g_mine, g_land,
-    pair_send, pair_recv, chip_send, chip_recv, half_send, half_recv,
+    pair_send, pair_recv, chip_send, chip_recv, half_send, half_recv, via_send, via_recv,
     *, across, depth_count, sharers,
 ):
     at = Place(across, depth_count)
@@ -141,71 +142,102 @@
         copy.start()
         return copy
 
-    def forward(which, offset, pair_copy):
-        pair_copy.wait_recv()
-
+    def add_rows(which, offset, source, slot, start, number):
         def body(i, carry):
-            here = pl.ds(pl.multiple_of(i * tile, tile), tile)
-            total = mine[which][offset, here, :].astype(jnp.float32) + take[which][
-                offset, here, :
+            here = pl.ds(pl.multiple_of(start + i * step, step), step)
+            total = mine[which][offset, here, :].astype(jnp.float32) + source[
+                slot, here, :
             ].astype(jnp.float32)
             mine[which][offset, here, :] = total.astype(dtype)
             return carry
 
-        lax.fori_loop(0, mine[which].shape[1] // tile, body, 0)
-        if offset == 0:
-            return None
-        chip, z = at.ahead(offset)
+        step = min(tile, number)
+        lax.fori_loop(0, number // step, body, 0)
+
+    def to_chip(which, offset, rows, slot, send_sem, recv_sem, target):
+        chip, z = at.ahead(target)
         copy = send(
-            mine[which].at[offset],
-            land[which].at[offset - 1],
-            chip_send.at[which, offset],
-            chip_recv.at[which, offset],
+            mine[which].at[offset, rows],
+            land[which].at[slot, rows],
+            send_sem,
+            recv_sem,
             at.device(chip, z, at.core),
         )
         copy.start()
         return copy
 
+    def forward(which, offset, pair_copy):
+        pair_copy.wait_recv()
+        rows = mine[which].shape[1]
+        add_rows(which, offset, take[which], offset, 0, rows)
+        if offset == 0:
+            return
+        if at.square and offset == 3:
+            via[which] = [
+                to_chip(
+                    which, 3, pl.ds(0, rows // 2), 2,
+                    chip_send.at[which, 3], chip_recv.at[which, 3], 1,
+                ),
+                to_chip(
+                    which, 3, pl.ds(rows // 2, rows // 2), 2,
+                    via_send.at[which], via_recv.at[which], 2,
+                ),
+            ]
+            return
+        if at.square:
+            passed = 2 - offset
+            via[which][passed].wait_recv()
+            add_rows(which, offset, land[which], 2, passed * (rows // 2), rows // 2)
+        direct[which].append(
+            to_chip(
+                which, offset, pl.ds(0, rows), offset - 1,
+                chip_send.at[which, offset], chip_recv.at[which, offset], offset,
+            )
+        )
+
     def finish(which, out):
         def body(i, carry):
             here = pl.ds(pl.multiple_of(i * tile, tile), tile)
             total = mine[which][0, here, :].astype(jnp.float32)
-            for other in range(at.count - 1):
+            for other in range(2 if at.square else at.count - 1):
                 total = total + land[which][other, here, :].astype(jnp.float32)
             out[here, :] = total.astype(dtype)
             return carry
 
         lax.fori_loop(0, mine[which].shape[1] // tile, body, 0)
 
-    offsets = list(range(1, at.count)) + [0]
-    steps = [(which, offset) for which in range(3) for offset in offsets]
-    pairs, chips = [], [[], [], []]
+    order = (1, 0, 2)
+    if at.square:
+        steps = [(1, 3), (2, 3), (0, 3)] + [(which, k) for which in order for k in (1, 2)]
+    else:
+        steps = [(which, k) for which in order for k in range(1, at.count)]
+    steps = steps + [(which, 0) for which in order]
+    pairs, via, direct = [], {}, ([], [], [])
     for which, offset in steps:
         pairs.append(compute(which, offset))
         done = len(pairs) - 2
         if done >= 0:
-            before, place = steps[done]
-            chips[before].append(forward(before, place, pairs[done]))
-    chips[2].append(forward(2, 0, pairs[-1]))
-
-    for copy in chips[0][:-1]:
+            forward(*steps[done], pairs[done])
+    forward(*steps[-1], pairs[-1])
+
+    for copy in direct[0]:
         copy.wait_recv()
     finish(0, kv_half)
     swap = send(kv_half, kv_other, half_send, half_recv, at.partner())
     swap.start()
-    for copy in chips[1][:-1]:
+    for copy in direct[1]:
         copy.wait_recv()
     finish(1, q_out)
     swap.wait()
     kv_out[pl.ds(pl.multiple_of(at.core * half, half), half), :] = kv_half[...]
     kv_out[pl.ds(pl.multiple_of((1 - at.core) * half, half), half), :] = kv_other[...]
-    for copy in chips[2][:-1]:
+    for copy in direct[2]:
         copy.wait_recv()
     finish(2, g_out)
     for copy in pairs:
         copy.wait_send()
-    for group in chips:
-        for copy in group[:-1]:
+    for which in range(3):
+        for copy in direct[which] + via.get(which, []):
             copy.wait_send()
 
 
@@ -238,7 +270,7 @@
         + buffers(block, columns)
         + buffers(block, columns)
         + [dma((3, count))] * 4
-        + [dma, dma],
+        + [dma, dma, dma((3,)), dma((3,))],
         compiler_params=pltpu.CompilerParams(
             vmem_limit_bytes=60 * 1024 * 1024, collective_id=0, has_side_effects=True
         ),
@@ -248,13 +280,14 @@
 
 def gather_kernel(*refs, number, across, depth_count):
     ins, outs = refs[:number], refs[number : 2 * number]
-    chip_send, chip_recv, pair_send, pair_recv, own_sem = refs[2 * number :]
+    chip_send, chip_recv, pair_send, pair_recv, own_sem, via_send, via_recv = refs[2 * number :]
     at = Place(across, depth_count)
     member = at.chip * 2 + at.core
     at.meet()
-    sends, chips, pairs, owns = [], {}, [], []
+    halves = [x.shape[0] // 2 for x in ins]
+    sends, pairs, owns = [], [], []
     for i in range(number):
-        for offset in range(1, at.count):
+        for offset in range(1, 3 if at.square else at.count):
             chip, z = at.ahead(offset)
             copy = send(
                 ins[i],
@@ -281,13 +314,43 @@
         for offset in range(1, at.count):
             chip, z = at.behind(offset)
             arrived = outs[i].at[chip * 2 + at.core, z]
-            send(
-                ins[i],
-                arrived,
-                chip_send.at[i, offset],
-                chip_recv.at[i, offset],
-                at.device(chip, z, at.core),
-            ).wait_recv()
+            if at.square and offset == 3:
+                for part, (send_sem, recv_sem) in enumerate(
+                    (
+                        (chip_send.at[i, 3], chip_recv.at[i, 3]),
+                        (via_send.at[i], via_recv.at[i]),
+                    )
+                ):
+                    piece = pl.ds(part * halves[i], halves[i])
+                    send(
+                        ins[i].at[piece],
+                        arrived.at[piece],
+                        send_sem,
+                        recv_sem,
+                        at.device(chip, z, at.core),
+                    ).wait_recv()
+            else:
+                send(
+                    ins[i],
+                    arrived,
+                    chip_send.at[i, offset],
+                    chip_recv.at[i, offset],
+                    at.device(chip, z, at.core),
+                ).wait_recv()
+                if at.square:
+                    piece = pl.ds((offset - 1) * halves[i], halves[i])
+                    next_chip, next_z = at.ahead(3 - offset)
+                    sems = (chip_send.at[i, 3], chip_recv.at[i, 3])
+                    if offset == 2:
+                        sems = (via_send.at[i], via_recv.at[i])
+                    copy = send(
+                        arrived.at[piece],
+                        arrived.at[piece],
+                        *sems,
+                        at.device(next_chip, next_z, at.core),
+                    )
+                    copy.start()
+                    sends.append(copy)
             copy = send(
                 arrived, arrived, pair_send.at[i, offset], pair_recv.at[i, offset], at.partner()
             )
@@ -319,7 +382,7 @@
         ),
         in_specs=[pl.BlockSpec(memory_space=pl.ANY)] * number,
         out_specs=(pl.BlockSpec(memory_space=pl.ANY),) * number,
-        scratch_shapes=[dma((number, count))] * 4 + [dma((number,))],
+        scratch_shapes=[dma((number, count))] * 4 + [dma((number,))] * 3,
         compiler_params=pltpu.CompilerParams(
             vmem_limit_bytes=VMEM_LIMIT, collective_id=collective_id, has_side_effects=True
         ),

time: 338 us -> 293 us (0.87)
  Pallas kernels: 313 us -> 262 us
  waiting for transfers between devices: 0.02 us -> 5.74 us
    pallas_call x2, Pallas kernels: 126 us -> 98.9 us  [gather(): pl.pallas_call(functools.partial(gather_kernel, number=number, across=acr...]
    pallas_call x1, Pallas kernels: 120 us -> 95.5 us  [project_sum(): pl.pallas_call(functools.partial(project_sum_kernel, across=across, depth...]
    reduce_scatter x1, waiting for transfers between devices: 0.01 us -> 5.72 us  [per_device(): input_grad = lax.psum_scatter(summed, 'gy', scatter_dimension=0, tiled=True)]
  transfers between devices with their start and end apart: 1 -> 1, of which waited for: 0 -> 1; matrix products, arithmetic and copies ran while one was open for 0% -> 0% of each run, Pallas kernels for 24% -> 24%
where the time goes in v3:
time: 293 us
  Pallas kernels  262 us (89%)
  between operations  14.1 us (5%)
  other arithmetic  8.72 us (3%)
  waiting for transfers between devices  5.74 us (2%)
    pallas_call x2, Pallas kernels, gather(): pl.pallas_call(functools.partial(gather_kernel, number=number, across=acr...  98.9 us
    pallas_call x1, Pallas kernels, project_sum(): pl.pallas_call(functools.partial(project_sum_kernel, across=across, depth...  95.5 us
    pallas_call x1, Pallas kernels, attend(): pl.pallas_call(functools.partial(attend_kernel, tile=min(256, rows)), gri...  19.9 us
    pallas_call x1, Pallas kernels, input_grad_part(): pl.pallas_call(input_grad_kernel, grid=(tokens // tile,), out_shape=jax.S...  18.4 us
    pallas_call x1, Pallas kernels, qkv_grads(): pl.pallas_call(qkv_grad_kernel, grid=(across,), out_shape=(jax.ShapeDtype...  16.1 us
    pallas_call x1, Pallas kernels, out_grad(): pl.pallas_call(out_grad_kernel, grid=(across,), out_shape=jax.ShapeDtypeS...  13.3 us
  transfers between devices with their start and end apart: 1, of which 1 were waited for; matrix products, arithmetic and copies ran while one was open for 0% of the time, Pallas kernels for 24%

profile of v3, /device:TPU:0, one launch (start us, length us, event | category | flops | bytes accessed | tf_op | source)
XLA Modules:
  0.0 292.5 jit_solution(7717334357844393574)
XLA Ops:
  7.2 0.0 reduce-scatter.2.cloned.1.call-start
  7.2 0.7 convert_element_type.2
  7.9 1.7 copy.13.seg_col
  9.6 1.9 fusion
  11.5 1.3 pad_maximum_fusion
  12.8 95.5 %shard_map.119 = (bf16[1024,512]{1,0:T(8,128)(2,1)}, bf16[1024,512]{1,0:T(8,128)(2,1)}, bf16[1024,256]{1,0:T(8,128)(2,1)}) custom-call(bf16[2048,1024]{1,0:T(8,128)(2,1)} %x_ref.3, bf16[2048,1024]{1,0:T(8,128)(2,1)} %g_ref.1, bf16[1024,2048]{1,0:T(8,128)(2,1)} %wq_ref.3, bf16[1024,256]{1,0:T(8,128)(2,1)} %wk_ref.3, bf16[1024,256]{1,0:T(8,128)(2,1)} %wv_ref.3, ...), custom_call_target="tpu_custom_call" | custom-call | flops 17179869184 | bytes 33554432 | tf_op jit(solution)/shard_map/pallas_call | solution.py:257
  108.4 19.9 %shard_map.120 = (bf16[1024,512]{1,0:T(8,128)(2,1)}, bf16[1024,512]{1,0:T(8,128)(2,1)}, bf16[1024,256]{1,0:T(8,128)(2,1)}) custom-call(bf16[1024,512]{1,0:T(8,128)(2,1)} %get-tuple-element.18.q_ref, bf16[1024,512]{1,0:T(8,128)(2,1)} %get-tuple-element.19.g_ref, bf16[1024,256]{1,0:T(8,128)(2,1)} %get-tuple-element.20.kv_ref, ...), custom_call_target="tpu_custom_call" | custom-call | flops 5368709120 | bytes 8388608 | tf_op jit(solution)/shard_map/pallas_call | solution.py:448
  128.3 56.9 %shard_map.121 = (bf16[4,2,1024,256]{3,2,1,0:T(8,128)(2,1)}, bf16[4,2,1024,512]{3,2,1,0:T(8,128)(2,1)}) custom-call(bf16[1024,256]{1,0:T(8,128)(2,1)} %get-tuple-element.22.refs_0_, bf16[1024,512]{1,0:T(8,128)(2,1)} %get-tuple-element.23.refs_1_), custom_call_target="tpu_custom_call" | custom-call | bytes 134217728 | tf_op jit(solution)/shard_map/pallas_call | solution.py:378
  185.2 4.8 %reduce_sum.12.dkv_ref = bf16[2,2048,256]{2,1,0:T(8,128)(2,1)} reduce(bf16[2,2,2048,256]{3,2,1,0:T(8,128)(2,1)} %bitcast.6, bf16[]{:T(256)} %constant.9.clone.1), dimensions={1}, to_apply=%region_0.0 | reduce | flops 1048576 | bytes 6291458 | tf_op jit(solution)/shard_map/reduce_sum | solution.py:613
  190.0 18.4 %shard_map.122 = bf16[2048,1024]{1,0:T(8,128)(2,1)} custom-call(bf16[4,2048,512]{2,1,0:T(8,128)(2,1)} %bitcast.9, bf16[2,2048,256]{2,1,0:T(8,128)(2,1)} %reduce_sum.12.dkv_ref, bf16[1024,2048]{1,0:T(8,128)(2,1)} %wq_ref.3, bf16[1024,256]{1,0:T(8,128)(2,1)} %wk_ref.3, bf16[1024,256]{1,0:T(8,128)(2,1)} %wv_ref.3), custom_call_target="tpu_custom_call" | custom-call | flops 10737418240 | bytes 16777216 | tf_op jit(solution)/shard_map/pallas_call | solution.py:498
  208.4 0.0 reduce-scatter.2.cloned.1.call-update
  208.5 42.1 %shard_map.124 = bf16[4,2,1024,512]{3,2,1,0:T(8,128)(2,1)} custom-call(bf16[1024,512]{1,0:T(8,128)(2,1)} %get-tuple-element.30.refs_0_), custom_call_target="tpu_custom_call" | custom-call | bytes 134217728 | tf_op jit(solution)/shard_map/pallas_call | solution.py:378
  250.5 13.3 %shard_map.125 = bf16[2048,1024]{1,0:T(8,128)(2,1)} custom-call(bf16[4,2048,512]{2,1,0:T(8,128)(2,1)} %bitcast.5, bf16[2048,1024]{1,0:T(8,128)(2,1)} %g_ref.1), custom_call_target="tpu_custom_call" | custom-call | flops 8589934592 | bytes 16777216 | tf_op jit(solution)/shard_map/pallas_call | solution.py:564
  263.8 16.1 %shard_map.123 = (bf16[1024,2048]{1,0:T(8,128)(2,1)}, bf16[1024,256]{1,0:T(8,128)(2,1)}, bf16[1024,256]{1,0:T(8,128)(2,1)}) custom-call(bf16[2048,1024]{1,0:T(8,128)(2,1)} %x_ref.3, bf16[4,2048,512]{2,1,0:T(8,128)(2,1)} %bitcast.10, bf16[2,2048,256]{2,1,0:T(8,128)(2,1)} %reduce_sum.12.dkv_ref), custom_call_target="tpu_custom_call" | custom-call | flops 10737418240 | bytes 16777216 | tf_op jit(solution)/shard_map/pallas_call | solution.py:533
  280.0 5.7 %reduce-scatter.2.cloned.1.call-done = bf16[512,1024]{1,0:T(8,128)(2,1)} async-done(((bf16[2048,1024]{1,0:T(8,128)(2,1)}), bf16[512,1024]{1,0:T(8,128)(2,1)}) %reduce-scatter.2.cloned.1.call-update) | async-done | bytes 1048592 | tf_op jit(solution)/shard_map/reduce_scatter | solution.py:619
  (1 shorter events, 0.0 us)
Async XLA Ops:
  7.2 278.5 %reduce-scatter.2.cloned.1.call-start = ((), (), s32[]{:S(2)}) async-start(), calls=%async_computation.1 | async-start | bytes 5242880 | tf_op jit(solution)/shard_map/reduce_scatter | solution.py:619
Sparse Core Ops, SparseCore 0:
  208.6 77.0 reduce-scatter.1
